TPU v7x, 32 devices: a whole 2x2x4 slice. The times are simulated.
32 devices in a mesh: box: 4 (over z), slab: 8 (over y, x, core).
Axes of the slice: x: 2, y: 2, z: 4, core: 2. Of those that a mesh axis runs over, the one named last changes fastest.
Arguments:
- hidden_field: bfloat16 [4, 8, 64, 128, 128], P('box', None, 'slab'), may hold values from -6 to 6
- cone_grad: float32 [256, 128, 128], P(('box', 'slab')), may hold values from -6 to 6
- conv_weight: bfloat16 [8, 27], replicated, may hold values from -0.4375 to 0.4375
- box_lower: int32 [256], P(('box', 'slab')), may hold values from 0 to 3, as said below
- box_upper: int32 [256], P(('box', 'slab')), may hold values from 0 to 3, as said below
- plane_lower: int32 [256], P(('box', 'slab')), may hold values from 0 to 63, as said below
- plane_upper: int32 [256], P(('box', 'slab')), may hold values from 0 to 63, as said below
- weight_lower: int32 [256], P(('box', 'slab')), may hold values from 0 to 256
- weight_upper: int32 [256], P(('box', 'slab')), may hold values from 0 to 256, as said below
Outputs:
- hidden_grad: bfloat16 [4, 8, 64, 128, 128], P('box', None, 'slab')
- weight_grad: float32 [8, 27], replicated
Inputs may be any that keep to these rules, and one draw needn't show every extreme that they name: With g = l // 64 the group of plane l, box_lower[l] is g or g - 1 (never below 0). box_upper[l] = min(box_lower[l] + 1, 3). Each box b has one offset o_b, and for one box, drawn from the seed, o_b = 32; plane_lower[l] = (l + o_b) mod 64 with b = box_lower[l]. plane_upper[l] = (l + o_b) mod 64 with b = box_upper[l], the same offsets. weight_upper[l] = 256 - weight_lower[l].
All inputs are finite; a program needn't handle non-finite values.
Results may differ from a plain program's by a relative error of at most 0.005.
Values may be sent and summed in bfloat16 or wider, within the bound.
A program may use at most 320 MiB of HBM per device.

v0:
```python
import math
import jax
import jax.numpy as jnp
from jax import lax
from jax.sharding import PartitionSpec as P

WDEN = 256


def passed_along(value, axis, steps):
    count = lax.axis_size(axis)
    first, last = (max(0, -steps), min(count, count - steps))
    return lax.ppermute(value, axis, [(source, source + steps) for source in range(first, last)])


def with_halo(cells, sides, width):
    for axis, dim in sides:
        count = lax.axis_size(axis)
        head = lax.slice_in_dim(cells, 0, width, axis=dim)
        tail = lax.slice_in_dim(cells, cells.shape[dim] - width, cells.shape[dim], axis=dim)
        cells = jnp.concatenate(
            [
                lax.ppermute(tail, axis, [(i, (i + 1) % count) for i in range(count)]),
                cells,
                lax.ppermute(head, axis, [((i + 1) % count, i) for i in range(count)]),
            ],
            axis=dim,
        )
    return cells


def wrap_sides(field):
    field = jnp.concatenate([field[:, -1:], field, field[:, :1]], 1)
    return jnp.concatenate([field[:, :, -1:], field, field[:, :, :1]], 2)


def local(
    hidden_field,
    cone_grad,
    conv_weight,
    box_lower,
    box_upper,
    plane_lower,
    plane_upper,
    weight_lower,
    weight_upper,
):
    group = lax.axis_index("box")
    column = lax.axis_index("slab")
    slab_count = lax.axis_size("slab")
    depth = cone_grad.shape[0]
    total_planes = depth * slab_count
    lower = weight_lower.astype(jnp.float32) / WDEN
    upper = weight_upper.astype(jnp.float32) / WDEN
    own_coef = jnp.where(box_lower == group, lower, 0.0) + jnp.where(box_upper == group, upper, 0.0)
    below_coef = jnp.where(box_lower == group - 1, lower, 0.0)
    above_coef = jnp.where(box_upper == group + 1, upper, 0.0)
    for_below = below_coef[:, None, None] * cone_grad
    for_above = above_coef[:, None, None] * cone_grad
    from_above = passed_along(for_below, "box", -1)
    from_below = passed_along(for_above, "box", 1)
    merged = (own_coef[:, None, None] * cone_grad + from_above + from_below).astype(jnp.bfloat16)
    first_plane = jnp.where(box_lower[0] == group, plane_lower[0], plane_upper[0])
    offset = (first_plane - column * depth) % total_planes
    whole = lax.all_gather(merged, "slab", axis=0, tiled=True)
    wanted = (column * depth + jnp.arange(depth, dtype=jnp.int32) - offset) % total_planes
    field_low = jnp.take(whole, wanted, axis=0)
    padded = with_halo(field_low, (("slab", 0),), 1)
    padded = wrap_sides(padded)[None, None]
    channel_count = hidden_field.shape[1]
    kernel = conv_weight.reshape(channel_count, 1, 3, 3, 3)[:, :, ::-1, ::-1, ::-1]
    numbers = ("NCDHW", "OIDHW", "NCDHW")
    hidden_grad = lax.conv_general_dilated(
        padded,
        kernel,
        (1, 1, 1),
        "VALID",
        dimension_numbers=numbers,
        preferred_element_type=jnp.float32,
    )
    hidden_grad = hidden_grad.astype(jnp.bfloat16).reshape(hidden_field.shape)
    as_kernel = hidden_field.reshape(
        channel_count, 1, depth, hidden_field.shape[3], hidden_field.shape[4]
    )
    partial_value = lax.conv_general_dilated(
        padded,
        as_kernel,
        (1, 1, 1),
        "VALID",
        dimension_numbers=numbers,
        preferred_element_type=jnp.float32,
    )
    partial_value = partial_value[0][:, ::-1, ::-1, ::-1].reshape(channel_count, 27)
    total = lax.psum(partial_value, ("box", "slab"))
    cells = lax.axis_size("box") * total_planes * field_low.shape[1] * field_low.shape[2]
    weight_grad = total * (1.0 / math.sqrt(cells))
    return (hidden_grad, weight_grad)


def solution(mesh):
    in_specs = (
        P("box", None, "slab", None, None),
        P(("box", "slab"), None, None),
        P(),
        P(("box", "slab")),
        P(("box", "slab")),
        P(("box", "slab")),
        P(("box", "slab")),
        P(("box", "slab")),
        P(("box", "slab")),
    )
    out_specs = (P("box", None, "slab", None, None), P())
    return jax.shard_map(local, mesh=mesh, in_specs=in_specs, out_specs=out_specs, check_vma=False)
```

profile of v0, /device:TPU:0, one launch (start us, length us, event | category | flops | bytes accessed | tf_op | source)
XLA Modules:
  0.0 805.5 jit_solution(18228177344446519526)
XLA Ops:
  7.2 0.0 copy-start.16
  7.2 0.0 copy-start.17
  7.2 0.0 copy-start.18
  7.2 0.0 all-gather.2.cloned.1.call-start
  7.2 0.7 fusion.3
  8.0 1.2 broadcast_multiply_fusion.1
  9.1 0.0 copy-start.6
  9.2 1.4 collective-permute-start
  10.6 5.6 collective-permute-start.1
  16.2 10.0 %collective-permute-done = f32[8,128,128]{2,1,0:T(8,128)S(1)} collective-permute-done((f32[8,128,128]{2,1,0:T(8,128)S(1)}, f32[8,128,128]{2,1,0:T(8,128)S(1)}, u32[]{:S(2)}, u32[]{:S(2)}) %collective-permute-start) | collective-permute-done | bytes 524320 | tf_op jit(solution)/shard_map/ppermute | solution.py:13
  26.1 1.2 collective-permute-done.1
  27.3 1.9 add_convert_fusion
  29.2 0.0 all-gather.2.cloned.1.call-update
  29.2 0.0 copy-done.16
  29.3 0.0 copy-done.17
  29.3 0.0 copy-done.18
  29.4 30.2 %all-gather.2.cloned.1.call-done = bf16[64,128,128]{2,1,0:T(8,128)(2,1)} async-done(((bf16[8,128,128]{2,1,0:T(8,128)(2,1)}), bf16[64,128,128]{2,1,0:T(8,128)(2,1)}) %all-gather.2.cloned.1.call-update) | async-done | bytes 2097168 | tf_op jit(solution)/shard_map/all_gather | solution.py:65
  59.6 2.2 gather_fusion
  61.8 0.1 broadcast_select_fusion
  61.9 0.0 copy-start
  61.9 0.3 collective-permute-start.2
  62.3 2.4 collective-permute-start.3
  64.6 0.0 copy-done.6
  64.6 69.5 %copy.41 = bf16[8,1,8,128,128]{0,1,4,3,2:T(2,128)(2,1)} copy(bf16[8,1,8,128,128]{4,3,2,0,1:T(8,128)(2,1)S(1)} %bitcast.34) | data formatting | bytes 4194304 | tf_op jit(solution)/shard_map/reshape | solution.py:82
  134.1 0.0 copy-done.14
  134.1 0.1 copy.36
  134.2 0.6 reshape.96
  134.9 0.0 collective-permute-done.2
  134.9 0.0 collective-permute-done.3
  134.9 0.0 copy-start.9
  134.9 0.0 copy-start.11
  134.9 0.0 copy-start.12
  134.9 0.1 pad_maximum_fusion.1
  135.0 0.2 fusion.7
  135.2 0.0 copy-start.2
  135.2 0.0 copy-start.4
  135.2 0.0 copy-done
  135.2 0.7 copy-done.2
  135.9 0.1 copy-done.4
  136.0 0.6 fusion.15
  136.6 0.0 copy-done.7
  136.6 0.0 copy-done.9
  136.6 184.9 %copy.40 = bf16[1,1,10,130,130]{1,0,4,3,2:T(2,128)(2,1)} copy(bf16[1,1,10,130,130]{4,3,2,1,0:T(8,128)(2,1)S(1)} %fusion.15) | data formatting | bytes 676000 | tf_op jit(solution)/shard_map/broadcast_in_dim | solution.py:69
  321.5 0.0 copy-done.11
  321.5 0.0 copy-done.12
  321.6 0.0 copy-start.5
  321.6 0.0 copy-start.8
  321.6 0.0 copy-start.10
  321.6 253.9 %fusion.9 = f32[1,8,3,3,3]{1,0,4,3,2:T(1,128)S(1)} fusion(bf16[1,1,10,130,130]{1,0,4,3,2:T(2,128)(2,1)} %copy.40, bf16[8,1,8,128,128]{0,1,4,3,2:T(2,128)(2,1)} %copy.41), kind=kOutput, calls=%fused_computation.40 | convolution fusion | flops 56623104 | bytes 2436016 | tf_op jit(solution)/shard_map/conv_general_dilated | solution.py:85
  575.5 39.6 %psum.7 = f32[8,27]{0,1:T(8,128)S(1)} all-reduce(f32[8,27]{0,1:T(8,128)S(1)} %reshape.75), channel_id=1, replica_groups=mesh['box'=4,'slab'=8] {'box','slab'}, use_global_device_ids=true, to_apply=%region_0.1 | all-reduce | flops 216 | bytes 1728 | tf_op jit(solution)/shard_map/psum | solution.py:94
  615.2 0.7 copy.43
  615.8 0.0 copy-done.5
  615.9 1.3 fusion.16
  617.1 0.4 copy.47
  617.5 0.1 pad.clone
  617.6 0.3 reshape.78
  618.0 0.4 fusion.2
  618.3 0.0 copy-start.13
  618.3 33.7 %copy.37 = bf16[1,10,130,8,19]{3,0,4,2,1:T(2,128)(2,1)} copy(bf16[1,10,130,8,19]{2,4,3,1,0:T(8,128)(2,1)S(1)} %fusion.2) | data formatting | bytes 790400 | tf_op jit(solution)/shard_map/conv_general_dilated | solution.py:73
  652.0 112.6 %fusion.10 = bf16[8,128,8,17,8]{4,2,3,1,0:T(8,128)(2,1)} fusion(bf16[1,10,130,8,19]{3,0,4,2,1:T(2,128)(2,1)} %copy.37, bf16[8,1,3,3,3]{0,1,4,3,2:T(2,128)(2,1)S(1)} %copy-done.13), kind=kOutput, calls=%fused_computation.41 | convolution fusion | flops 60162048 | bytes 2623856 | tf_op jit(solution)/shard_map/conv_general_dilated | solution.py:73
  764.6 30.5 %copy.39 = bf16[8,128,8,17,8]{1,4,3,2,0:T(8,128)(2,1)S(1)} copy(bf16[8,128,8,17,8]{4,2,3,1,0:T(8,128)(2,1)} %fusion.10) | data formatting | bytes 4456448 | tf_op jit(solution)/shard_map/conv_general_dilated | solution.py:73
  795.1 0.5 select_convert_fusion
  795.7 0.1 slice_bitcast_fusion
  795.8 2.9 copy.42
  (21 shorter events, 0.2 us)
Async XLA Ops:
  7.2 22.1 %copy-start.16 = (s32[8]{0:T(128)S(1)}, s32[8]{0:T(128)}, u32[]{:S(2)}) copy-start(s32[8]{0:T(128)} %param.12) | copy-start | bytes 100
  7.2 22.1 %copy-start.17 = (s32[8]{0:T(128)S(1)}, s32[8]{0:T(128)}, u32[]{:S(2)}) copy-start(s32[8]{0:T(128)} %param.14) | copy-start | bytes 100
  7.2 22.1 %copy-start.18 = (s32[8]{0:T(128)S(1)}, s32[8]{0:T(128)}, u32[]{:S(2)}) copy-start(s32[8]{0:T(128)} %param.15) | copy-start | bytes 100
  7.2 52.4 %all-gather.2.cloned.1.call-start = ((), (), s32[]{:S(2)}) async-start(), calls=%async_computation | async-start | bytes 2359296 | tf_op jit(solution)/shard_map/all_gather | solution.py:65
  9.1 55.5 %copy-start.6 = (bf16[1,8,8,128,128]{4,3,2,1,0:T(8,128)(2,1)S(1)}, bf16[1,8,8,128,128]{4,3,2,1,0:T(8,128)(2,1)}, u32[]{:S(2)}) copy-start(bf16[1,8,8,128,128]{4,3,2,1,0:T(8,128)(2,1)} %param.9) | copy-start | bytes 6291460
  9.2 17.0 %collective-permute-start = (f32[8,128,128]{2,1,0:T(8,128)S(1)}, f32[8,128,128]{2,1,0:T(8,128)S(1)}, u32[]{:S(2)}, u32[]{:S(2)}) collective-permute-start(f32[8,128,128]{2,1,0:T(8,128)S(1)} %get-tuple-element.8), channel_id=1, source_target_pairs={{8,0},{16,8},{24,16},{9,1},{17,9},{25,17},{10,2},{18,10},{26,18},{... | collective-permute-start | bytes 1572872 | tf_op jit(solution)/shard_map/ppermute | solution.py:13
  10.6 16.7 %collective-permute-start.1 = (f32[8,128,128]{2,1,0:T(8,128)S(1)}, f32[8,128,128]{2,1,0:T(8,128)S(1)}, u32[]{:S(2)}, u32[]{:S(2)}) collective-permute-start(f32[8,128,128]{2,1,0:T(8,128)S(1)} %get-tuple-element.9), channel_id=1, source_target_pairs={{0,8},{8,16},{16,24},{1,9},{9,17},{17,25},{2,10},{10,18},{18,26},{... | collective-permute-start | bytes 1572872 | tf_op jit(solution)/shard_map/ppermute | solution.py:13
  61.9 73.3 %copy-start = (bf16[8,128,128]{2,1,0:T(8,128)(2,1)}, bf16[8,128,128]{2,1,0:T(8,128)(2,1)S(1)}, u32[]{:S(2)}) copy-start(bf16[8,128,128]{2,1,0:T(8,128)(2,1)S(1)} %broadcast_select_fusion) | copy-start | bytes 786436
  61.9 72.9 %collective-permute-start.2 = (bf16[1,128,128]{2,1,0:T(8,128)(2,1)S(1)}, bf16[1,128,128]{2,1,0:T(8,128)(2,1)S(1)}, u32[]{:S(2)}, u32[]{:S(2)}) collective-permute-start(bf16[1,128,128]{2,1,0:T(8,128)(2,1)S(1)} %get-tuple-element.14), channel_id=1, source_target_pairs={{0,1},{1,2},{2,3},{3,4},{4,5},{5,6},{6,7},{7,0},{8,9},{9,10},{10,1... | collective-permute-start | bytes 98312 | tf_op jit(solution)/shard_map/ppermute | solution.py:23
  62.3 72.6 %collective-permute-start.3 = (bf16[1,128,128]{2,1,0:T(8,128)(2,1)S(1)}, bf16[1,128,128]{2,1,0:T(8,128)(2,1)S(1)}, u32[]{:S(2)}, u32[]{:S(2)}) collective-permute-start(bf16[1,128,128]{2,1,0:T(8,128)(2,1)S(1)} %get-tuple-element.15), channel_id=1, source_target_pairs={{1,0},{2,1},{3,2},{4,3},{5,4},{6,5},{7,6},{0,7},{9,8},{10,9},{11,1... | collective-permute-start | bytes 98312 | tf_op jit(solution)/shard_map/ppermute | solution.py:25
  64.6 69.5 %copy-start.14 = (bf16[8,27]{1,0:T(8,128)(2,1)S(1)}, bf16[8,27]{1,0:T(8,128)(2,1)}, u32[]{:S(2)}) copy-start(bf16[8,27]{1,0:T(8,128)(2,1)} %param.11) | copy-start | bytes 1300
  134.9 1.8 copy-start.7
  134.9 1.8 copy-start.9
  134.9 186.7 %copy-start.11 = (bf16[10,1,128]{2,1,0:T(2,128)(2,1)}, bf16[10,1,128]{2,1,0:T(2,128)(2,1)S(1)}, u32[]{:S(2)}) copy-start(bf16[10,1,128]{2,1,0:T(2,128)(2,1)S(1)} %get-tuple-element.12) | copy-start | bytes 7684
  134.9 186.6 %copy-start.12 = (bf16[10,1,128]{2,1,0:T(2,128)(2,1)}, bf16[10,1,128]{2,1,0:T(2,128)(2,1)S(1)}, u32[]{:S(2)}) copy-start(bf16[10,1,128]{2,1,0:T(2,128)(2,1)S(1)} %get-tuple-element.13) | copy-start | bytes 7684
  135.2 0.7 copy-start.2
  135.2 0.8 copy-start.4
  321.6 294.3 %copy-start.1 = (bf16[8,128,128]{2,1,0:T(8,128)(2,1)S(1)}, bf16[8,128,128]{2,1,0:T(8,128)(2,1)}, u32[]{:S(2)}) copy-start(bf16[8,128,128]{2,1,0:T(8,128)(2,1)} %copy-done) | copy-start | bytes 786436
  321.6 294.3 %copy-start.3 = (bf16[10,130,1]{2,1,0:T(8,128)(2,1)S(1)}, bf16[10,130,1]{2,1,0:T(8,128)(2,1)}, u32[]{:S(2)}) copy-start(bf16[10,130,1]{2,1,0:T(8,128)(2,1)} %copy-done.2) | copy-start | bytes 7804
  321.6 294.3 %copy-start.5 = (bf16[10,130,1]{2,1,0:T(8,128)(2,1)S(1)}, bf16[10,130,1]{2,1,0:T(8,128)(2,1)}, u32[]{:S(2)}) copy-start(bf16[10,130,1]{2,1,0:T(8,128)(2,1)} %copy-done.4) | copy-start | bytes 7804
  321.6 294.3 %copy-start.8 = (bf16[1,128,128]{2,1,0:T(8,128)(2,1)S(1)}, bf16[1,128,128]{2,1,0:T(8,128)(2,1)}, u32[]{:S(2)}) copy-start(bf16[1,128,128]{2,1,0:T(8,128)(2,1)} %copy-done.7) | copy-start | bytes 98308
  321.6 294.3 %copy-start.10 = (bf16[1,128,128]{2,1,0:T(8,128)(2,1)S(1)}, bf16[1,128,128]{2,1,0:T(8,128)(2,1)}, u32[]{:S(2)}) copy-start(bf16[1,128,128]{2,1,0:T(8,128)(2,1)} %copy-done.9) | copy-start | bytes 98308
  618.3 33.7 %copy-start.13 = (bf16[8,1,3,3,3]{0,1,4,3,2:T(2,128)(2,1)S(1)}, bf16[8,1,3,3,3]{0,1,4,3,2:T(2,128)(2,1)}, u32[]{:S(2)}) copy-start(bf16[8,1,3,3,3]{0,1,4,3,2:T(2,128)(2,1)} %reshape.96) | copy-start | bytes 1300
  764.6 30.5 %copy-start.15 = (pred[8,17]{1,0:T(8,128)(4,1)S(1)}, pred[8,17]{1,0:T(8,128)(4,1)}, u32[]{:S(2)}) copy-start(pred[8,17]{1,0:T(8,128)(4,1)} %constant.70) | copy-start | bytes 412
Sparse Core Ops, SparseCore 0:
  29.3 30.2 all-gather.1
where the time goes:
time: 806 us
  matrix products  366 us (45%)
  local copies, waits for them, and re-layouts  327 us (41%)
  waiting for transfers between devices  41.4 us (5%)
  blocking collectives  39.6 us (5%)
  between operations  14.5 us (2%)
  starting transfers between devices  9.75 us (1%)
    conv_general_dilated x1, matrix products, local(): lax.conv_general_dilated(padded, as_kernel, (1, 1, 1), 'VALID', dimension...  254 us
    broadcast_in_dim x2, local copies, waits for them, and re-layouts, local(): padded = wrap_sides(padded)[None, None]  185 us
    conv_general_dilated x1, matrix products, local(): lax.conv_general_dilated(padded, kernel, (1, 1, 1), 'VALID', dimension_nu...  113 us
    reshape x1, local copies, waits for them, and re-layouts, local(): hidden_field.reshape(channel_count, 1, depth, hidden_field.shape[3], hidd...  69.5 us
    conv_general_dilated x4, local copies, waits for them, and re-layouts, local(): lax.conv_general_dilated(padded, kernel, (1, 1, 1), 'VALID', dimension_nu...  64.5 us
    psum x1, blocking collectives, local(): total = lax.psum(partial_value, ('box', 'slab'))  39.6 us
    all_gather x1, waiting for transfers between devices, local(): whole = lax.all_gather(merged, 'slab', axis=0, tiled=True)  30.2 us
  transfers between devices with their start and end apart: 5, of which 3 were waited for; matrix products, arithmetic and copies ran while one was open for 9% of the time, Pallas kernels for 0%

commit v1 on v0

--- a/solution.py
+++ b/solution.py
@@ -62,7 +62,12 @@
     merged = (own_coef[:, None, None] * cone_grad + from_above + from_below).astype(jnp.bfloat16)
     first_plane = jnp.where(box_lower[0] == group, plane_lower[0], plane_upper[0])
     offset = (first_plane - column * depth) % total_planes
-    whole = lax.all_gather(merged, "slab", axis=0, tiled=True)
+    ring = [merged]
+    for hop in range(7):
+        ring.append(lax.ppermute(ring[-1], "slab", [(dev, (dev + 1) % 8) for dev in range(8)]))
+    whole = jnp.roll(
+        jnp.concatenate(ring[::-1], axis=0), (lax.axis_index("slab") + 1) * ring[0].shape[0], axis=0
+    )
     wanted = (column * depth + jnp.arange(depth, dtype=jnp.int32) - offset) % total_planes
     field_low = jnp.take(whole, wanted, axis=0)
     padded = with_halo(field_low, (("slab", 0),), 1)

time: 806 us -> 833 us (1.033); the launches traced: 806 us -> 824 us
  local copies, waits for them, and re-layouts: 327 us -> 343 us
  waiting for transfers between devices: 41.4 us -> 55.9 us
  between operations: 14.5 us -> 3.04 us
    ppermute x0 -> x7, waiting for transfers between devices: none -> 44.8 us  [local(): lax.ppermute(ring[-1], 'slab', [(dev, (dev + 1) % 8) for dev in range(8)])]
    all_gather x1 -> x0, waiting for transfers between devices: 30.2 us -> none  [local(): whole = lax.all_gather(merged, 'slab', axis=0, tiled=True)]
    reshape x1, local copies, waits for them, and re-layouts: 69.5 us -> 86.2 us  [local(): hidden_field.reshape(channel_count, 1, depth, hidden_field.shape[3], hidd...]
  transfers between devices with their start and end apart: 5 -> 11, of which waited for: 3 -> 9; matrix products, arithmetic and copies ran while one was open for 9% -> 11% of each run, Pallas kernels for 0% -> 0%
where the time goes in v1:
time: 833 us; the launch traced here: 824 us
  matrix products  367 us (44%)
  local copies, waits for them, and re-layouts  343 us (41%)
  waiting for transfers between devices  55.9 us (7%)
  blocking collectives  41.8 us (5%)
    conv_general_dilated x1, matrix products, local(): lax.conv_general_dilated(padded, as_kernel, (1, 1, 1), 'VALID', dimension...  254 us
    broadcast_in_dim x2, local copies, waits for them, and re-layouts, local(): padded = wrap_sides(padded)[None, None]  185 us
    conv_general_dilated x1, matrix products, local(): lax.conv_general_dilated(padded, kernel, (1, 1, 1), 'VALID', dimension_nu...  113 us
    reshape x1, local copies, waits for them, and re-layouts, local(): hidden_field.reshape(channel_count, 1, depth, hidden_field.shape[3], hidd...  86.2 us
    conv_general_dilated x4, local copies, waits for them, and re-layouts, local(): lax.conv_general_dilated(padded, kernel, (1, 1, 1), 'VALID', dimension_nu...  64.5 us
    ppermute x7, waiting for transfers between devices, local(): lax.ppermute(ring[-1], 'slab', [(dev, (dev + 1) % 8) for dev in range(8)])  44.8 us
    psum x1, blocking collectives, local(): total = lax.psum(partial_value, ('box', 'slab'))  41.8 us
  transfers between devices with their start and end apart: 11, of which 9 were waited for; matrix products, arithmetic and copies ran while one was open for 11% of the time, Pallas kernels for 0%

profile of v1, /device:TPU:0, one launch (start us, length us, event | category | flops | bytes accessed | tf_op | source)
XLA Modules:
  0.0 824.0 jit_solution(11572275763911845006)
XLA Ops:
  0.6 0.7 fusion.3
  1.4 1.2 broadcast_multiply_fusion.1
  2.5 1.3 collective-permute-start
  3.8 5.6 collective-permute-start.1
  9.4 10.0 %collective-permute-done = f32[8,128,128]{2,1,0:T(8,128)S(1)} collective-permute-done((f32[8,128,128]{2,1,0:T(8,128)S(1)}, f32[8,128,128]{2,1,0:T(8,128)S(1)}, u32[]{:S(2)}, u32[]{:S(2)}) %collective-permute-start) | collective-permute-done | bytes 524320 | tf_op jit(solution)/shard_map/ppermute | solution.py:13
  19.4 1.2 collective-permute-done.1
  20.6 1.2 add_convert_fusion
  21.8 0.1 collective-permute-start.2
  21.8 6.7 collective-permute-done.2
  28.5 0.0 collective-permute-start.3
  28.5 6.7 collective-permute-done.3
  35.2 0.0 collective-permute-start.4
  35.2 6.7 collective-permute-done.4
  41.9 0.0 collective-permute-start.5
  41.9 6.7 collective-permute-done.5
  48.6 0.0 collective-permute-start.6
  48.6 6.7 collective-permute-done.6
  55.3 0.0 collective-permute-start.7
  57.3 4.7 collective-permute-done.7
  62.0 0.0 collective-permute-start.8
  62.1 6.6 collective-permute-done.8
  69.4 0.1 constant_dynamic-slice_fusion
  69.5 0.6 gather_fusion
  70.1 0.1 broadcast_select_fusion
  70.2 0.0 copy-start
  70.2 0.1 collective-permute-start.10
  70.3 0.5 collective-permute-start.9
  70.8 86.2 %copy.31 = bf16[8,1,8,128,128]{0,1,4,3,2:T(2,128)(2,1)} copy(bf16[8,1,8,128,128]{4,3,2,0,1:T(8,128)(2,1)} %bitcast.34) | data formatting | bytes 4194304 | tf_op jit(solution)/shard_map/reshape | solution.py:87
  157.0 0.0 copy-done.13
  157.0 0.1 copy.26
  157.1 0.6 reshape.96
  157.7 0.0 collective-permute-done.10
  157.7 0.0 collective-permute-done.9
  157.7 0.0 copy-start.7
  157.7 0.0 copy-start.8
  157.7 0.0 copy-start.10
  157.8 0.1 pad_maximum_fusion.1
  157.9 0.2 fusion.7
  158.0 0.0 copy-start.4
  158.1 0.3 copy-done.8
  158.3 0.0 copy-done.10
  158.3 0.4 copy-done.2
  158.8 0.1 copy-done.4
  158.9 0.6 fusion.15
  159.4 184.9 %copy.30 = bf16[1,1,10,130,130]{1,0,4,3,2:T(2,128)(2,1)} copy(bf16[1,1,10,130,130]{4,3,2,1,0:T(8,128)(2,1)S(1)} %fusion.15) | data formatting | bytes 676000 | tf_op jit(solution)/shard_map/broadcast_in_dim | solution.py:74
  344.4 0.0 copy-start.5
  344.4 0.0 copy-start.9
  344.4 0.0 copy-start.11
  344.4 254.1 %fusion.9 = f32[1,8,3,3,3]{1,0,4,3,2:T(1,128)S(1)} fusion(bf16[1,1,10,130,130]{1,0,4,3,2:T(2,128)(2,1)} %copy.30, bf16[8,1,8,128,128]{0,1,4,3,2:T(2,128)(2,1)} %copy.31), kind=kOutput, calls=%fused_computation.57 | convolution fusion | flops 56623104 | bytes 2436016 | tf_op jit(solution)/shard_map/conv_general_dilated | solution.py:90
  598.6 41.8 %psum.7 = f32[8,27]{0,1:T(8,128)S(1)} all-reduce(f32[8,27]{0,1:T(8,128)S(1)} %reshape.75), channel_id=1, replica_groups=mesh['box'=4,'slab'=8] {'box','slab'}, use_global_device_ids=true, to_apply=%region_0.1 | all-reduce | flops 216 | bytes 1728 | tf_op jit(solution)/shard_map/psum | solution.py:99
  640.4 0.7 copy.33
  641.1 0.0 copy-done.9
  641.1 0.0 copy-done.11
  641.1 1.3 fusion.16
  642.4 0.4 copy.37
  642.8 0.1 pad.clone
  642.9 0.3 reshape.78
  643.3 0.4 fusion.2
  643.6 33.7 %copy.27 = bf16[1,10,130,8,19]{3,0,4,2,1:T(2,128)(2,1)} copy(bf16[1,10,130,8,19]{2,4,3,1,0:T(8,128)(2,1)S(1)} %fusion.2) | data formatting | bytes 790400 | tf_op jit(solution)/shard_map/conv_general_dilated | solution.py:78
  677.3 112.6 %fusion.10 = bf16[8,128,8,17,8]{4,2,3,1,0:T(8,128)(2,1)} fusion(bf16[1,10,130,8,19]{3,0,4,2,1:T(2,128)(2,1)} %copy.27, bf16[8,1,3,3,3]{0,1,4,3,2:T(2,128)(2,1)S(1)} %copy-done.12), kind=kOutput, calls=%fused_computation.58 | convolution fusion | flops 60162048 | bytes 2623856 | tf_op jit(solution)/shard_map/conv_general_dilated | solution.py:78
  789.9 30.5 %copy.29 = bf16[8,128,8,17,8]{1,4,3,2,0:T(8,128)(2,1)S(1)} copy(bf16[8,128,8,17,8]{4,2,3,1,0:T(8,128)(2,1)} %fusion.10) | data formatting | bytes 4456448 | tf_op jit(solution)/shard_map/conv_general_dilated | solution.py:78
  820.4 0.5 select_convert_fusion
  821.0 0.1 slice_bitcast_fusion
  821.1 2.9 copy.32
  (41 shorter events, 0.7 us)
Async XLA Ops:
  2.5 16.8 %collective-permute-start = (f32[8,128,128]{2,1,0:T(8,128)S(1)}, f32[8,128,128]{2,1,0:T(8,128)S(1)}, u32[]{:S(2)}, u32[]{:S(2)}) collective-permute-start(f32[8,128,128]{2,1,0:T(8,128)S(1)} %get-tuple-element.6), channel_id=1, source_target_pairs={{8,0},{16,8},{24,16},{9,1},{17,9},{25,17},{10,2},{18,10},{26,18},{... | collective-permute-start | bytes 1572872 | tf_op jit(solution)/shard_map/ppermute | solution.py:13
  3.8 16.7 %collective-permute-start.1 = (f32[8,128,128]{2,1,0:T(8,128)S(1)}, f32[8,128,128]{2,1,0:T(8,128)S(1)}, u32[]{:S(2)}, u32[]{:S(2)}) collective-permute-start(f32[8,128,128]{2,1,0:T(8,128)S(1)} %get-tuple-element.7), channel_id=1, source_target_pairs={{0,8},{8,16},{16,24},{1,9},{9,17},{17,25},{2,10},{10,18},{18,26},{... | collective-permute-start | bytes 1572872 | tf_op jit(solution)/shard_map/ppermute | solution.py:13
  21.8 6.7 collective-permute-start.2
  28.5 6.7 collective-permute-start.3
  35.2 6.7 collective-permute-start.4
  41.9 6.7 collective-permute-start.5
  48.6 6.7 collective-permute-start.6
  55.3 6.7 collective-permute-start.7
  62.0 6.7 collective-permute-start.8
  70.2 87.8 %copy-start = (bf16[8,128,128]{2,1,0:T(8,128)(2,1)}, bf16[8,128,128]{2,1,0:T(8,128)(2,1)S(1)}, u32[]{:S(2)}) copy-start(bf16[8,128,128]{2,1,0:T(8,128)(2,1)S(1)} %broadcast_select_fusion) | copy-start | bytes 786436
  70.2 87.4 %collective-permute-start.10 = (bf16[1,128,128]{2,1,0:T(8,128)(2,1)S(1)}, bf16[1,128,128]{2,1,0:T(8,128)(2,1)S(1)}, u32[]{:S(2)}, u32[]{:S(2)}) collective-permute-start(bf16[1,128,128]{2,1,0:T(8,128)(2,1)S(1)} %get-tuple-element.13), channel_id=1, source_target_pairs={{1,0},{2,1},{3,2},{4,3},{5,4},{6,5},{7,6},{0,7},{9,8},{10,9},{11,1... | collective-permute-start | bytes 98312 | tf_op jit(solution)/shard_map/ppermute | solution.py:25
  70.3 87.4 %collective-permute-start.9 = (bf16[1,128,128]{2,1,0:T(8,128)(2,1)S(1)}, bf16[1,128,128]{2,1,0:T(8,128)(2,1)S(1)}, u32[]{:S(2)}, u32[]{:S(2)}) collective-permute-start(bf16[1,128,128]{2,1,0:T(8,128)(2,1)S(1)} %get-tuple-element.12), channel_id=1, source_target_pairs={{0,1},{1,2},{2,3},{3,4},{4,5},{5,6},{6,7},{7,0},{8,9},{9,10},{10,1... | collective-permute-start | bytes 98312 | tf_op jit(solution)/shard_map/ppermute | solution.py:23
  70.8 86.2 %copy-start.13 = (bf16[8,27]{1,0:T(8,128)(2,1)S(1)}, bf16[8,27]{1,0:T(8,128)(2,1)}, u32[]{:S(2)}) copy-start(bf16[8,27]{1,0:T(8,128)(2,1)} %param.11) | copy-start | bytes 1300
  157.7 186.7 %copy-start.6 = (bf16[1,128,128]{2,1,0:T(8,128)(2,1)}, bf16[1,128,128]{2,1,0:T(8,128)(2,1)S(1)}, u32[]{:S(2)}) copy-start(bf16[1,128,128]{2,1,0:T(8,128)(2,1)S(1)} %collective-permute-done.10) | copy-start | bytes 98308
  157.7 186.7 %copy-start.7 = (bf16[1,128,128]{2,1,0:T(8,128)(2,1)}, bf16[1,128,128]{2,1,0:T(8,128)(2,1)S(1)}, u32[]{:S(2)}) copy-start(bf16[1,128,128]{2,1,0:T(8,128)(2,1)S(1)} %collective-permute-done.9) | copy-start | bytes 98308
  157.7 0.6 copy-start.8
  157.7 0.6 copy-start.10
  158.0 0.7 copy-start.2
  158.0 0.8 copy-start.4
  344.4 296.7 %copy-start.1 = (bf16[8,128,128]{2,1,0:T(8,128)(2,1)S(1)}, bf16[8,128,128]{2,1,0:T(8,128)(2,1)}, u32[]{:S(2)}) copy-start(bf16[8,128,128]{2,1,0:T(8,128)(2,1)} %copy-done) | copy-start | bytes 786436
  344.4 296.7 %copy-start.3 = (bf16[10,130,1]{2,1,0:T(8,128)(2,1)S(1)}, bf16[10,130,1]{2,1,0:T(8,128)(2,1)}, u32[]{:S(2)}) copy-start(bf16[10,130,1]{2,1,0:T(8,128)(2,1)} %copy-done.2) | copy-start | bytes 7804
  344.4 296.7 %copy-start.5 = (bf16[10,130,1]{2,1,0:T(8,128)(2,1)S(1)}, bf16[10,130,1]{2,1,0:T(8,128)(2,1)}, u32[]{:S(2)}) copy-start(bf16[10,130,1]{2,1,0:T(8,128)(2,1)} %copy-done.4) | copy-start | bytes 7804
  344.4 296.7 %copy-start.9 = (bf16[10,1,128]{2,1,0:T(2,128)(2,1)S(1)}, bf16[10,1,128]{2,1,0:T(2,128)(2,1)}, u32[]{:S(2)}) copy-start(bf16[10,1,128]{2,1,0:T(2,128)(2,1)} %copy-done.8) | copy-start | bytes 7684
  344.4 296.7 %copy-start.11 = (bf16[10,1,128]{2,1,0:T(2,128)(2,1)S(1)}, bf16[10,1,128]{2,1,0:T(2,128)(2,1)}, u32[]{:S(2)}) copy-start(bf16[10,1,128]{2,1,0:T(2,128)(2,1)} %copy-done.10) | copy-start | bytes 7684
  643.6 33.7 %copy-start.12 = (bf16[8,1,3,3,3]{0,1,4,3,2:T(2,128)(2,1)S(1)}, bf16[8,1,3,3,3]{0,1,4,3,2:T(2,128)(2,1)}, u32[]{:S(2)}) copy-start(bf16[8,1,3,3,3]{0,1,4,3,2:T(2,128)(2,1)} %reshape.96) | copy-start | bytes 1300
  789.9 30.5 %copy-start.14 = (pred[8,17]{1,0:T(8,128)(4,1)S(1)}, pred[8,17]{1,0:T(8,128)(4,1)}, u32[]{:S(2)}) copy-start(pred[8,17]{1,0:T(8,128)(4,1)} %constant.86) | copy-start | bytes 412
